TPU v7x, 32 devices: a whole 2x2x4 slice. The times are simulated.
32 devices in a mesh: row: 8 (over z, y), col: 4 (over x, core).
Axes of the slice: x: 2, y: 2, z: 4, core: 2. Of those that a mesh axis runs over, the one named last changes fastest.
Arguments:
- object_field: float32 [2, 2048, 1024], P(None, 'row', 'col'), may hold values from -5 to 5
- probe: float32 [2, 256, 256], replicated, may hold values from -6 to 6
- amplitudes: float32 [8, 4, 4, 256, 256], P('row', 'col'), may hold values from 0 to 11, as said below
- positions: int32 [8, 4, 4, 2], P('row', 'col'), may hold values from 0 to 64
Outputs:
- object_next: float32 [2, 2048, 1024], P(None, 'row', 'col')
- probe_next: float32 [2, 256, 256], replicated
Inputs may be any that keep to these rules, and one draw needn't show every extreme that they name: Positive amplitudes.
All inputs are finite; a program needn't handle non-finite values.
Results may differ from a plain program's by a relative error of at most 0.0003.
Values sent between devices are 32-bit elements; how exact they have to be, the bound alone decides.
No kernel may reach another device: no remote copies, remote signals or barrier semaphores. Data moves between devices by JAX's collectives and lax.ppermute only.
A program may use at most 64 MiB of HBM per device.

v0:
```python
import functools
import math

import jax
import jax.numpy as jnp
import numpy as np
from jax import lax
from jax.experimental import pallas as pl
from jax.experimental.pallas import tpu as pltpu
from jax.sharding import PartitionSpec as P

MARGIN = 32
LANES = 128
SUBLANES = 8

smoothing = 0.1
regular = 1.0
epsilon = 1e-06

f32 = jnp.float32
bf16 = jnp.bfloat16


def tables(length):
    half = length // 2
    scaling = 1.0 / math.sqrt(length)
    k = np.arange(half)
    phases = (k[:, None] * k[None, :] % half) * (2.0 * math.pi / half)
    cosine, sine = np.cos(phases) * scaling, np.sin(phases) * scaling
    right = np.block([[cosine, -sine], [sine, cosine]])
    left = np.block([[cosine, sine], [-sine, cosine]])
    both = np.stack([left, right]).astype(np.float32)
    high = both.astype(bf16)
    low = (both - high.astype(np.float32)).astype(bf16)
    matrices = np.stack([high, low], 1)
    angle = k * (2.0 * math.pi / length)
    turn = np.stack([np.cos(angle), np.sin(angle)]).astype(np.float32)
    rows = np.broadcast_to(turn[:, :, None], (2, half, LANES)).copy()
    columns = np.broadcast_to(turn[:, None, :], (2, SUBLANES, half)).copy()
    return matrices, rows, columns


def split(x):
    high = x.astype(bf16)
    return high, (x - high.astype(f32)).astype(bf16)


def dot(a, b):
    return jnp.dot(a, b, preferred_element_type=f32)


def times_matrix(data, matrix):
    high, low = split(data)
    return dot(
        jnp.concatenate([high, low, high], 1),
        jnp.concatenate([matrix[0], matrix[0], matrix[1]], 0),
    )


def matrix_times(matrix, data):
    high, low = split(data)
    return dot(
        jnp.concatenate([matrix[0], matrix[0], matrix[1]], 1),
        jnp.concatenate([high, low, high], 0),
    )


def turned(real, imag, cosine, sine):
    return real * cosine - imag * sine, real * sine + imag * cosine


def pack(chunks, lane, width):
    place = lax.broadcasted_iota(jnp.int32, chunks[0].shape, 1) // width
    out = jnp.zeros_like(chunks[0])
    for q, chunk in enumerate(chunks):
        shift = (q * width - lane) % LANES
        moved = pltpu.roll(chunk, shift, 1) if shift else chunk
        out = jnp.where(place == q, moved, out)
    return out


def pack_rows(rows, lane, width):
    count = rows.shape[0] * width // LANES
    return pack([rows[q : q + count] for q in range(0, rows.shape[0], count)], lane, width)


def unpack(packed, q, lane, width):
    shift = (lane - q * width) % LANES
    moved = pltpu.roll(packed, shift, 1) if shift else packed
    place = lax.broadcasted_iota(jnp.int32, packed.shape, 1)
    return jnp.where((place >= lane) & (place < lane + width), moved, 0.0)


def unpack_rows(packed, lane, width):
    return jnp.concatenate([unpack(packed, q, lane, width) for q in range(LANES // width)], 0)


def lifted(tile, shift):
    groups = tile.shape[0] // SUBLANES
    turned_rows = pltpu.roll(
        tile.reshape(groups, SUBLANES, LANES), lax.rem(SUBLANES - shift, SUBLANES), 1
    )
    place = lax.broadcasted_iota(jnp.int32, (groups - 1, SUBLANES, LANES), 1)
    picked = jnp.where(place < SUBLANES - shift, turned_rows[:-1], turned_rows[1:])
    return picked.reshape((groups - 1) * SUBLANES, LANES)


def lowered(tile, shift):
    groups = tile.shape[0] // SUBLANES
    moved = pltpu.roll(tile.reshape(groups, SUBLANES, LANES), shift, 1)
    none = jnp.zeros((1, SUBLANES, LANES), f32)
    place = lax.broadcasted_iota(jnp.int32, (groups + 1, SUBLANES, LANES), 1)
    picked = jnp.where(
        place >= shift, jnp.concatenate([moved, none], 0), jnp.concatenate([none, moved], 0)
    )
    return picked.reshape((groups + 1) * SUBLANES, LANES)


def spot(offsets, f, margin, taller):
    a, b = offsets[f, 0], offsets[f, 1]
    shift = lax.rem(a, SUBLANES)
    lane = b + LANES - margin
    tile = lane // LANES
    return pl.ds(pl.multiple_of(a - shift, SUBLANES), taller), shift, tile, lane - tile * LANES


def window_of(padded, plane, spot_of, tiles):
    at, shift, base, lane = spot_of
    moved = [
        pltpu.roll(padded[plane, base + t, at, :], lax.rem(LANES - lane, LANES), 1)
        for t in range(tiles + 1)
    ]
    place = lax.broadcasted_iota(jnp.int32, moved[0].shape, 1)
    parts = [
        lifted(jnp.where(place < LANES - lane, moved[t], moved[t + 1]), shift)
        for t in range(tiles)
    ]
    return jnp.concatenate(parts, 1)


def add_window(work, term, spot_of):
    at, shift, base, lane = spot_of
    tiles = term.shape[1] // LANES
    moved = [
        pltpu.roll(lowered(term[:, t * LANES : (t + 1) * LANES], shift), lane, 1)
        for t in range(tiles)
    ]
    none = jnp.zeros_like(moved[0])
    place = lax.broadcasted_iota(jnp.int32, none.shape, 1)
    for t in range(tiles + 1):
        here = moved[t] if t < tiles else none
        before = moved[t - 1] if t else none
        work[base + t, at, :] += jnp.where(place >= lane, here, before)


def neighbours(first, second, index, count):
    even = index % 2 == 0
    before = jnp.where(even, second, first)
    after = jnp.where(even, first, second)
    return jnp.where(index > 0, before, 0.0), jnp.where(index < count - 1, after, 0.0)


def pack_kernel(margin, place, field, columns_first, columns_second):
    planes, side, _ = field.shape
    even = place[2] % 2 == 0
    for plane in range(planes):
        left = pack_rows(field[plane, :, :LANES], 0, margin)
        right = pack_rows(field[plane, :, side - LANES :], LANES - margin, margin)
        columns_first[plane] = jnp.where(even, right, left)
        columns_second[plane] = jnp.where(even, left, right)


def prepare_kernel(margin, offsets, amplitude, probe, sorted_out, total_out, powers, held):
    frames, length, _ = amplitude.shape
    half = length // 2
    power = probe[0] * probe[0] + probe[1] * probe[1]
    powers[...] = jnp.zeros(powers.shape, f32)
    for f in range(frames):
        add_window(powers, power, spot(offsets, f, margin, length + SUBLANES))
    row = lax.broadcasted_iota(jnp.int32, (length, length), 0)
    column = lax.broadcasted_iota(jnp.int32, (length, length), 1)
    source = jnp.where(column < half, 2 * column, 2 * (column - half) + 1)
    order = jnp.where(row == source, 1.0, 0.0).astype(bf16)
    total = jnp.zeros((SUBLANES, length), f32)
    for f in range(frames):
        values = amplitude[f]
        total += jnp.sum((values * values).reshape(length // SUBLANES, SUBLANES, length), 0)
        high = values.astype(bf16)
        rest = values - high.astype(f32)
        middle = rest.astype(bf16)
        low = (rest - middle.astype(f32)).astype(bf16)
        placed = dot(high, order) + (dot(middle, order) + dot(low, order))
        for parity in range(2):
            held[f, parity] = placed[:, parity * half : (parity + 1) * half]
            for start in range(2):
                at = 2 * parity + start
                sorted_out[f, at * half : (at + 1) * half, :] = held[
                    f, parity, pl.ds(start, half, stride=2), :
                ]
    total_out[...] = sum(total[:, t * LANES : (t + 1) * LANES] for t in range(length // LANES))


def corner_kernel(counts, place, first, second, inner_first, inner_second, above, below, out):
    planes, margin, side = first.shape
    inner = inner_first.shape[1]
    even = place[2] % 2 == 0
    for plane in range(planes):
        before, after = neighbours(first[plane], second[plane], place[1], counts[0])
        above[plane] = before
        below[plane] = after
        both = jnp.concatenate([before, after], 0)
        left = pack_rows(both[:, :LANES], 0, margin)
        right = pack_rows(both[:, side - LANES :], LANES - margin, margin)
        out[plane, :inner] = inner_first[plane]
        out[plane, inner:] = jnp.where(even, right, left)
        out[planes + plane, :inner] = inner_second[plane]
        out[planes + plane, inner:] = jnp.where(even, left, right)


def transform_pair(waves, row_turn, column_turn, matrices, amplitudes):
    length = waves[0][0].shape[0]
    half = length // 2
    row_cos, row_sin = row_turn
    column_cos, column_sin = column_turn

    mixed = []
    for real, imag in waves:
        odd = turned(real[:half] - real[half:], imag[:half] - imag[half:], row_cos, -row_sin)
        stacked = jnp.concatenate(
            [
                jnp.concatenate([real[:half] + real[half:], imag[:half] + imag[half:]], 0),
                jnp.concatenate(odd, 0),
            ],
            1,
        )
        mixed.append(matrix_times(matrices.at[0], stacked))

    far = []
    for value in mixed:
        evens, odds = [], []
        for parity in range(2):
            part = value[:, parity * length : (parity + 1) * length]
            real, imag = part[:half], part[half:]
            evens.append(
                jnp.concatenate(
                    [real[:, :half] + real[:, half:], imag[:, :half] + imag[:, half:]], 1
                )
            )
            odd = turned(
                real[:, :half] - real[:, half:],
                imag[:, :half] - imag[:, half:],
                column_cos,
                -column_sin,
            )
            odds.append(jnp.concatenate(odd, 1))
        far.append(times_matrix(jnp.concatenate(evens + odds, 0), matrices.at[1]))

    turned_back = []
    for value, amplitude in zip(far, amplitudes):
        real, imag = value[:, :half], value[:, half:]
        factor = amplitude * lax.rsqrt(real * real + imag * imag + smoothing)
        corrected = jnp.concatenate([real * factor, imag * factor], 1)
        turned_back.append(times_matrix(corrected, matrices.at[0]))

    near = []
    for value in turned_back:
        even, odd = value[:length], value[length:]
        odd_real, odd_imag = turned(odd[:, :half], odd[:, half:], column_cos, column_sin)
        even_real, even_imag = even[:, :half], even[:, half:]
        real = jnp.concatenate([even_real + odd_real, even_real - odd_real], 1)
        imag = jnp.concatenate([even_imag + odd_imag, even_imag - odd_imag], 1)
        stacked = jnp.concatenate(
            [
                jnp.concatenate([real[:half], imag[:half]], 0),
                jnp.concatenate([real[half:], imag[half:]], 0),
            ],
            1,
        )
        near.append(matrix_times(matrices.at[1], stacked))

    results = []
    for value in near:
        even, odd = value[:, :length], value[:, length:]
        odd_real, odd_imag = turned(odd[:half], odd[half:], row_cos, row_sin)
        results.append(
            (
                jnp.concatenate([even[:half] + odd_real, even[:half] - odd_real], 0),
                jnp.concatenate([even[half:] + odd_imag, even[half:] - odd_imag], 0),
            )
        )
    return results


def frames_kernel(
    counts,
    blocks,
    place,
    offsets,
    field,
    above,
    below,
    columns_first,
    columns_second,
    probe,
    amplitude,
    total,
    powers,
    matrices,
    row_turn,
    column_turn,
    work,
    kept,
    sent,
    padded,
    sums,
):
    frames = amplitude.shape[0]
    length = probe.shape[1]
    side = field.shape[1]
    margin = above.shape[1]
    reach = side + 2 * margin
    taller = length + SUBLANES
    per = LANES // margin
    inner = side // per
    tiles = length // LANES
    last = side // LANES + 1

    for plane in range(2):
        for tile in range(side // LANES):
            lanes = pl.ds(tile * LANES, LANES)
            padded[plane, tile + 1, :margin, :] = above[plane, :, lanes]
            padded[plane, tile + 1, margin : margin + side, :] = field[plane, :, lanes]
            padded[plane, tile + 1, margin + side : reach, :] = below[plane, :, lanes]
        left, right = neighbours(
            columns_first[plane], columns_second[plane], place[2], counts[1]
        )
        for tile, packed, lane in ((0, left, LANES - margin), (last, right, 0)):
            corners = unpack_rows(packed[inner:], lane, margin)
            padded[plane, tile, :margin, :] = corners[:margin]
            padded[plane, tile, margin : margin + side, :] = unpack_rows(
                packed[:inner], lane, margin
            )
            padded[plane, tile, margin + side : reach, :] = corners[margin:]
        padded[plane, :, reach:, :] = jnp.zeros((last + 1, SUBLANES, LANES), f32)
    work[...] = jnp.zeros(work.shape, f32)
    first = jnp.where(place[1] + place[2] == 0, 1.0, 0.0).astype(f32)
    sums[0] = probe[0] * first
    sums[1] = probe[1] * first
    sums[2] = jnp.full((length, length), regular, f32) * first

    row_cos, row_sin = (jnp.concatenate([row_turn[k]] * tiles, 1) for k in range(2))
    column_cos, column_sin = (column_turn[k, 0:1, :] for k in range(2))
    together = max(k for k in (1, 2, 4) if frames % k == 0)

    def visit(step, carry):
        chosen = [step * together + k for k in range(together)]
        spots = [spot(offsets, f, margin, taller) for f in chosen]
        windows = [
            tuple(window_of(padded, plane, spot_of, tiles) for plane in range(2))
            for spot_of in spots
        ]
        probe_real, probe_imag = probe[0], probe[1]
        waves = [
            (
                probe_real * real - probe_imag * imag,
                probe_real * imag + probe_imag * real,
            )
            for real, imag in windows
        ]
        nears = transform_pair(
            waves,
            (row_cos, row_sin),
            (column_cos, column_sin),
            matrices,
            [amplitude[f] for f in chosen],
        )
        for (window_real, window_imag), (near_real, near_imag), spot_of in zip(
            windows, nears, spots
        ):
            sums[0] += window_real * near_real + window_imag * near_imag
            sums[1] += window_real * near_imag - window_imag * near_real
            sums[2] += window_real * window_real + window_imag * window_imag
            add_window(work.at[0], probe_real * near_real + probe_imag * near_imag, spot_of)
            add_window(work.at[1], probe_real * near_imag - probe_imag * near_real, spot_of)
        return carry

    lax.fori_loop(0, frames // together, visit, 0)

    rows = length // blocks
    half_rows = blocks // 2 * 3 * tiles * rows
    for p in range(blocks):
        out, q, base = (
            (kept, p, place[0]) if p < blocks // 2 else (sent, p - blocks // 2, place[3])
        )
        source = pl.multiple_of((base ^ q) * rows, rows)
        for plane in range(3):
            for tile in range(tiles):
                start = ((3 * q + plane) * tiles + tile) * rows
                out[start : start + rows, :] = sums[
                    plane, pl.ds(source, rows), pl.ds(tile * LANES, LANES)
                ]
    kept[half_rows:, :] = total[...]
    sent[half_rows : half_rows + SUBLANES, :] = total[...]
    even = place[2] % 2 == 0
    start = half_rows + SUBLANES
    depth = reach // per
    for plane in range(3):
        canvas = powers if plane == 2 else work.at[plane]
        right = pack_rows(canvas[last, :reach, :], 0, margin)
        left = pack_rows(canvas[0, :reach, :], LANES - margin, margin)
        at = start + plane * depth
        sent[at : at + depth, :] = jnp.where(even, right, left)
        at += 3 * depth
        sent[at : at + depth, :] = jnp.where(even, left, right)


def row_edge_kernel(counts, margin, place, work, powers, first, second, out):
    planes = work.shape[0] + 1
    tiles = work.shape[1] - 2
    reach = work.shape[2] - SUBLANES
    depth = first.shape[0] // planes
    even = place[1] % 2 == 0
    for plane in range(planes):
        canvas = powers if plane == planes - 1 else work.at[plane]
        at = pl.ds(plane * depth, depth)
        before, after = neighbours(first[at, :], second[at, :], place[2], counts[1])
        last = LANES // margin - 1
        edges = []
        for begin, chunk, cut in (
            (0, 0, slice(None, margin)),
            (reach - margin, last, slice(depth - margin, None)),
        ):
            parts = [canvas[tile + 1, begin : begin + margin, :] for tile in range(tiles)]
            parts[0] += unpack(before, chunk, 0, margin)[cut]
            parts[-1] += unpack(after, chunk, LANES - margin, margin)[cut]
            edges.append(parts)
        for tile in range(tiles):
            at = pl.ds((plane * tiles + tile) * margin, margin)
            out[at, :] = jnp.where(even, edges[1][tile], edges[0][tile])
            at = pl.ds(((planes + plane) * tiles + tile) * margin, margin)
            out[at, :] = jnp.where(even, edges[0][tile], edges[1][tile])


def object_kernel(
    counts, margin, place, field, work, powers, first, second, row_first, row_second, out
):
    planes = work.shape[0] + 1
    tiles = work.shape[1] - 2
    side = field.shape[1]
    depth = first.shape[0] // planes
    for tile in range(tiles):
        lanes = pl.ds(tile * LANES, LANES)
        total = []
        for plane in range(planes):
            canvas = powers if plane == planes - 1 else work.at[plane]
            at = pl.ds((plane * tiles + tile) * margin, margin)
            above, below = neighbours(row_first[at, :], row_second[at, :], place[1], counts[0])
            part = canvas[tile + 1, margin : margin + side, :]
            at = pl.ds(plane * depth, depth)
            before, after = neighbours(first[at, :], second[at, :], place[2], counts[1])
            if tile == 0:
                part += unpack_rows(before, 0, margin)[margin : margin + side]
            if tile == tiles - 1:
                part += unpack_rows(after, LANES - margin, margin)[margin : margin + side]
            part = jnp.concatenate(
                [
                    part[:margin] + above,
                    part[margin : side - margin],
                    part[side - margin :] + below,
                ],
                0,
            )
            total.append(part)
        weight = 1.0 / (total[2] + regular)
        out[0, :, lanes] = (field[0, :, lanes] + total[0]) * weight
        out[1, :, lanes] = (field[1, :, lanes] + total[1]) * weight


def probe_kernel(frame_count, blocks, place, stepped, total, out):
    planes, length, _ = out.shape
    tiles = length // LANES
    rows = length // blocks
    values = stepped[...]
    power = jnp.sum(values * values)
    target = jnp.sum(total[...]) / frame_count
    scale = jnp.sqrt(jnp.full((rows, LANES), target / (power + epsilon), f32))
    for p in range(blocks):
        base, q = (place[0], p) if p < blocks // 2 else (place[3], p - blocks // 2)
        home = pl.multiple_of((base ^ q) * rows, rows)
        for plane in range(planes):
            for tile in range(tiles):
                start = ((planes * p + plane) * tiles + tile) * rows
                out[plane, pl.ds(home, rows), pl.ds(tile * LANES, LANES)] = (
                    values[start : start + rows] * scale
                )


def shape(*dims):
    return jax.ShapeDtypeStruct(dims, f32)


def call(kernel, outputs, scalars=0, operands=0, scratch=(), cost=None):
    vmem = pl.BlockSpec(memory_space=pltpu.VMEM)
    smem = pl.BlockSpec(memory_space=pltpu.SMEM)
    return pl.pallas_call(
        kernel,
        out_shape=outputs,
        in_specs=[smem] * scalars + [vmem] * operands,
        out_specs=jax.tree.map(lambda _: vmem, outputs),
        scratch_shapes=list(scratch),
        cost_estimate=cost,
        compiler_params=pltpu.CompilerParams(vmem_limit_bytes=40 * 1024 * 1024),
    )


def paired(block, axis, first):
    count = lax.axis_size(axis)
    target = list(range(count))
    for i in range(first, count - 1, 2):
        target[i], target[i + 1] = i + 1, i
    return lax.ppermute(block, axis, list(enumerate(target)))


def relayed(block, axis):
    count = lax.axis_size(axis)
    target = {i: i + 2 if i % 2 == 0 else i - 2 for i in range(count)}
    target[count - 2], target[1] = count - 1, 0
    return lax.ppermute(block, axis, list(target.items()))


def exchanged(block, orders, distance):
    count = lax.axis_size("row") * lax.axis_size("col")
    masks = [
        sum(1 << bit for k, bit in enumerate(order) if distance >> k & 1) for order in orders
    ]
    return lax.ppermute(block, ("row", "col"), [(i, i ^ masks[i % 2]) for i in range(count)])


def per_device(object_field, probe, amplitudes, positions):
    planes, side, _ = object_field.shape
    length = probe.shape[1]
    margin = MARGIN
    reach = side + 2 * margin
    per = LANES // margin
    tiles = length // LANES
    measured = amplitudes[0, 0]
    frames = measured.shape[0]
    counts = lax.axis_size("row"), lax.axis_size("col")
    row = lax.axis_index("row").astype(jnp.int32)
    col = lax.axis_index("col").astype(jnp.int32)
    index = row * counts[1] + col
    col_bits = (counts[1] - 1).bit_length()
    across = list(range(1, col_bits))
    along = list(range(col_bits, col_bits + (counts[0] - 1).bit_length()))
    halvings = 2
    orders = tuple(
        order[:halvings] + order[halvings:][::-1] for order in (across + along, along[::-1] + across)
    )
    blocks = 2 << halvings
    rows = length // blocks
    homes = [
        sum(((index >> order[k]) & 1) << k for k in range(halvings))
        for order in orders
    ]
    core = index & 1
    homes[1] += blocks // 2
    place = jnp.stack(
        [
            jnp.where(core == 0, homes[0], homes[1]),
            row,
            col,
            jnp.where(core == 0, homes[1], homes[0]),
        ]
    )

    edge_rows = shape(planes, margin, side)
    inner = shape(planes, side // per, LANES)
    odd = row & 1
    last = side - margin
    rows_first = lax.dynamic_slice_in_dim(object_field, last - odd * last, margin, 1)
    rows_second = lax.dynamic_slice_in_dim(object_field, odd * last, margin, 1)
    rows_second = paired(rows_second, "row", 1)
    rows_first = paired(rows_first, "row", 0)
    inner_first, inner_second = call(
        functools.partial(pack_kernel, margin), (inner, inner), scalars=1, operands=1
    )(place, object_field)
    above, below, columns = call(
        functools.partial(corner_kernel, counts),
        (edge_rows, edge_rows, shape(2 * planes, reach // per, LANES)),
        scalars=1,
        operands=4,
    )(place, rows_first, rows_second, inner_first, inner_second)
    columns = paired(columns, "col", 0)
    relay = relayed(columns[planes:], "col")

    ordered, total, powers = call(
        functools.partial(prepare_kernel, margin),
        (
            shape(frames, 2 * length, length // 2),
            shape(SUBLANES, LANES),
            shape(side // LANES + 2, reach + SUBLANES, LANES),
        ),
        scalars=1,
        operands=2,
        scratch=(pltpu.VMEM((frames, 2, length, length // 2), f32),),
        cost=pl.CostEstimate(flops=10**9, bytes_accessed=2 * measured.size * 4, transcendentals=0),
    )(positions[0, 0], measured, probe)
    matrices, row_turn, column_turn = tables(length)
    half_rows = blocks // 2 * 3 * tiles * rows
    depth = 3 * reach // per
    work, kept, sent = call(
        functools.partial(frames_kernel, counts, blocks),
        (
            shape(2, side // LANES + 2, reach + SUBLANES, LANES),
            shape(half_rows + SUBLANES, LANES),
            shape(half_rows + SUBLANES + 2 * depth, LANES),
        ),
        scalars=2,
        operands=12,
        scratch=(
            pltpu.VMEM((2, side // LANES + 2, reach + SUBLANES, LANES), f32),
            pltpu.VMEM((3, length, length), f32),
        ),
    )(
        place,
        positions[0, 0],
        object_field,
        above,
        below,
        columns,
        relay,
        probe,
        ordered,
        total,
        powers,
        jnp.asarray(matrices),
        jnp.asarray(row_turn),
        jnp.asarray(column_turn),
    )

    arrived = paired(sent, "col", 0)
    current = kept + arrived[: half_rows + SUBLANES]
    first = arrived[half_rows + SUBLANES : half_rows + SUBLANES + depth]
    second = relayed(arrived[half_rows + SUBLANES + depth :], "col")
    block = 3 * tiles * rows
    total = current[-SUBLANES:]
    quarters = [
        jnp.concatenate([current[d * block : (d + 1) * block], total], 0) for d in range(blocks // 2)
    ]
    terms = [exchanged(quarters[d], orders, d) for d in range(2, blocks // 2)]
    near_quarter, second = lax.optimization_barrier((quarters[1], second))
    terms = [quarters[0], exchanged(near_quarter, orders, 1)] + terms
    while len(terms) > 1:
        terms = [terms[k] + terms[k + 1] for k in range(0, len(terms), 2)]
    current = terms[0]
    count = 3 * tiles * margin
    edges = call(
        functools.partial(row_edge_kernel, counts, margin),
        shape(2 * count, LANES),
        scalars=1,
        operands=4,
    )(place, work, powers, first, second)
    current, edges = lax.optimization_barrier((current, edges))
    edges = paired(edges, "row", 0)
    for step in range(halvings, len(orders[0])):
        if step == halvings + 1:
            current, edges = lax.optimization_barrier((current, edges))
            row_first = edges[:count]
            row_second = relayed(edges[count:], "row")
        current = current + exchanged(current, orders, 1 << step)
    size = tiles * rows
    weight = current[2 * size : 3 * size]
    stepped = current[: 2 * size] / jnp.concatenate([weight, weight], 0)
    stepped = jnp.concatenate(
        [stepped] + [exchanged(stepped, orders, d) for d in range(1, blocks // 2)], 0
    )
    object_next = call(
        functools.partial(object_kernel, counts, margin),
        shape(*object_field.shape),
        scalars=1,
        operands=7,
    )(place, object_field, work, powers, first, second, row_first, row_second)
    stepped = jnp.concatenate([stepped, paired(stepped, "col", 0)], 0)
    frame_count = frames * counts[0] * counts[1]
    probe_next = call(
        functools.partial(probe_kernel, frame_count, blocks),
        shape(*probe.shape),
        scalars=1,
        operands=2,
    )(place, stepped, current[3 * size :])
    return (object_next, probe_next)


def solution(mesh):
    return jax.shard_map(
        per_device,
        mesh=mesh,
        in_specs=(
            P(None, "row", "col"),
            P(),
            P("row", "col", None, None, None),
            P("row", "col", None, None),
        ),
        out_specs=(P(None, "row", "col"), P()),
        check_vma=False,
    )
```

profile of v0, /device:TPU:0, one launch (start us, length us, event | category | flops | bytes accessed | tf_op | source)
XLA Modules:
  0.0 58.7 jit_solution(2219095882977410359)
XLA Ops:
  0.6 0.9 %constant_dynamic-slice_fusion = (f32[2,32,256]{2,1,0:T(8,128)S(1)}, f32[2,32,256]{2,1,0:T(8,128)S(1)}) fusion(f32[2,256,256]{2,1,0:T(8,128)} %field.5, s32[]{:T(128)S(6)} %select_n.16, s32[]{:T(128)S(6)} %select_n.15), kind=kLoop, calls=%fused_computation.14 | loop fusion | bytes 262152 | tf_op jit(solution)/shard_map/dynamic_slice | solution.py:581
  1.5 0.7 %collective-permute-start.1 = (f32[2,32,256]{2,1,0:T(8,128)S(1)}, f32[2,32,256]{2,1,0:T(8,128)S(1)}, u32[]{:S(2)}, u32[]{:S(2)}) collective-permute-start(f32[2,32,256]{2,1,0:T(8,128)S(1)} %get-tuple-element.40), channel_id=1, source_target_pairs={{0,0},{4,8},{8,4},{12,16},{16,12},{20,24},{24,20},{28,28},{1,1},{5... | collective-permute-start | bytes 196616 | tf_op jit(solution)/shard_map/ppermute | solution.py:521
  2.2 5.8 %collective-permute-start = (f32[2,32,256]{2,1,0:T(8,128)S(1)}, f32[2,32,256]{2,1,0:T(8,128)S(1)}, u32[]{:S(2)}, u32[]{:S(2)}) collective-permute-start(f32[2,32,256]{2,1,0:T(8,128)S(1)} %get-tuple-element.41), channel_id=1, source_target_pairs={{0,4},{4,0},{8,12},{12,8},{16,20},{20,16},{24,28},{28,24},{1,5},{5... | collective-permute-start | bytes 196616 | tf_op jit(solution)/shard_map/ppermute | solution.py:521
  8.1 1.0 %copy-done = f32[2,256,256]{2,1,0:T(8,128)S(1)} copy-done((f32[2,256,256]{2,1,0:T(8,128)S(1)}, f32[2,256,256]{2,1,0:T(8,128)}, u32[]{:S(2)}) %copy-start) | copy-done | bytes 524312
  9.1 0.7 %shard_map.86 = (f32[2,64,128]{2,1,0:T(8,128)S(1)}, f32[2,64,128]{2,1,0:T(8,128)S(1)}) custom-call(s32[4]{0:T(128)S(1)} %pad_add_fusion.place, f32[2,256,256]{2,1,0:T(8,128)S(1)} %copy-done), custom_call_target="tpu_custom_call" | custom-call | tf_op jit(solution)/shard_map/pallas_call | solution.py:584
  9.8 0.4 collective-permute-done.first
  10.2 0.6 %shard_map.87 = (f32[2,32,256]{2,1,0:T(8,128)S(1)}, f32[2,32,256]{2,1,0:T(8,128)S(1)}, f32[4,80,128]{2,1,0:T(8,128)S(1)}) custom-call(s32[4]{0:T(128)S(1)} %pad_add_fusion.place, f32[2,32,256]{2,1,0:T(8,128)S(1)} %collective-permute-done.first, f32[2,32,256]{2,1,0:T(8,128)S(1)} %collective-permute-done.1.second, ...), custom_call_target="tpu_custom_call" | custom-call | tf_op jit(solution)/shard_map/pallas_call | solution.py:587
  11.0 0.8 %copy.10.offsets = s32[4,2]{1,0:T(4,128)S(1)} copy(s32[4,2]{0,1:T(2,128)} %bitcast.7) | data formatting | bytes 64 | tf_op jit(solution)/shard_map/squeeze | solution.py:626
  11.7 0.6 %collective-permute-done.2.columns_first = f32[4,80,128]{2,1,0:T(8,128)S(1)} collective-permute-done((f32[4,80,128]{2,1,0:T(8,128)S(1)}, f32[4,80,128]{2,1,0:T(8,128)S(1)}, u32[]{:S(2)}, u32[]{:S(2)}) %collective-permute-start.2) | collective-permute-done | bytes 163872 | tf_op jit(solution)/shard_map/ppermute | solution.py:521
  12.4 1.5 %collective-permute-start.3 = (f32[2,80,128]{2,1,0:T(8,128)S(1)}, f32[2,80,128]{2,1,0:T(8,128)S(1)}, u32[]{:S(2)}, u32[]{:S(2)}) collective-permute-start(f32[2,80,128]{2,1,0:T(8,128)S(1)} %slice.54), channel_id=1, source_target_pairs={{0,2},{1,0},{2,3},{3,1},{4,6},{5,4},{6,7},{7,5},{8,10},{9,8},{10,1... | collective-permute-start | bytes 245768 | tf_op jit(solution)/shard_map/ppermute | solution.py:528
  13.9 1.0 %copy-done.2 = f32[2,256,256]{2,1,0:T(8,128)S(1)} copy-done((f32[2,256,256]{2,1,0:T(8,128)S(1)}, f32[2,256,256]{2,1,0:T(8,128)}, u32[]{:S(2)}) %copy-start.2) | copy-done | bytes 524312
  14.9 1.2 %copy-done.6 = f32[1,1,4,256,256]{4,3,2,1,0:T(8,128)S(1)} copy-done((f32[1,1,4,256,256]{4,3,2,1,0:T(8,128)S(1)}, f32[1,1,4,256,256]{4,3,2,1,0:T(8,128)}, u32[]{:S(2)}) %copy-start.6) | copy-done | bytes 1048600
  16.1 1.5 %shard_map.88 = (f32[4,512,128]{2,1,0:T(8,128)S(1)}, f32[8,128]{1,0:T(8,128)S(1)}, f32[4,328,128]{2,1,0:T(8,128)S(1)}) custom-call(s32[4,2]{1,0:T(4,128)S(1)} %copy.10.offsets, f32[4,256,256]{2,1,0:T(8,128)S(1)} %bitcast.6, f32[2,256,256]{2,1,0:T(8,128)S(1)} %copy-done.2), custom_call_target="tpu_custom_call" | custom-call | flops 1000000000 | bytes 2097152 | tf_op jit(solution)/shard_map/pallas_call | solution.py:596
  17.7 6.8 %shard_map.89 = (f32[2,4,328,128]{3,2,1,0:T(8,128)S(1)}, f32[776,128]{1,0:T(8,128)S(1)}, f32[1256,128]{1,0:T(8,128)S(1)}) custom-call(s32[4]{0:T(128)S(1)} %pad_add_fusion.place, s32[4,2]{1,0:T(4,128)S(1)} %copy.10.offsets, f32[2,256,256]{2,1,0:T(8,128)S(1)} %copy-done.1, f32[2,32,256]{2,1,0:T(8,128)S(1)} %get-tuple-element.21.above, ...), custom_call_target="tpu_custom_call" | custom-call | tf_op jit(solution)/shard_map/pallas_call | solution.py:611
  24.6 2.1 %collective-permute-done.4 = f32[1256,128]{1,0:T(8,128)S(1)} collective-permute-done((f32[1256,128]{1,0:T(8,128)S(1)}, f32[1256,128]{1,0:T(8,128)S(1)}, u32[]{:S(2)}, u32[]{:S(2)}) %collective-permute-start.4) | collective-permute-done | bytes 643104 | tf_op jit(solution)/shard_map/ppermute | solution.py:521
  26.7 0.6 %collective-permute-start.5 = (f32[240,128]{1,0:T(8,128)S(1)}, f32[240,128]{1,0:T(8,128)S(1)}, u32[]{:S(2)}, u32[]{:S(2)}) collective-permute-start(f32[240,128]{1,0:T(8,128)S(1)} %get-tuple-element.38), channel_id=1, source_target_pairs={{0,2},{1,0},{2,3},{3,1},{4,6},{5,4},{6,7},{7,5},{8,10},{9,8},{10,1... | collective-permute-start | bytes 368648 | tf_op jit(solution)/shard_map/ppermute | solution.py:528
  27.4 2.3 %collective-permute-start.7 = (f32[200,128]{1,0:T(8,128)S(1)}, f32[200,128]{1,0:T(8,128)S(1)}, u32[]{:S(2)}, u32[]{:S(2)}) collective-permute-start(f32[200,128]{1,0:T(8,128)S(1)} %get-tuple-element.47), channel_id=1, source_target_pairs={{0,4},{1,9},{2,6},{3,11},{4,0},{5,13},{6,2},{7,15},{8,12},{9,1},{1... | collective-permute-start | bytes 307208 | tf_op jit(solution)/shard_map/ppermute | solution.py:536
  29.8 2.4 %collective-permute-start.6 = (f32[200,128]{1,0:T(8,128)S(1)}, f32[200,128]{1,0:T(8,128)S(1)}, u32[]{:S(2)}, u32[]{:S(2)}) collective-permute-start(f32[200,128]{1,0:T(8,128)S(1)} %get-tuple-element.31), channel_id=1, source_target_pairs={{0,2},{1,17},{2,0},{3,19},{4,6},{5,21},{6,4},{7,23},{8,10},{9,25},... | collective-permute-start | bytes 307208 | tf_op jit(solution)/shard_map/ppermute | solution.py:536
  32.2 0.6 %shard_map.90 = f32[384,128]{1,0:T(8,128)S(1)} custom-call(s32[4]{0:T(128)S(1)} %pad_add_fusion.place, f32[2,4,328,128]{3,2,1,0:T(8,128)S(1)} %get-tuple-element.27.work, f32[4,328,128]{2,1,0:T(8,128)S(1)} %get-tuple-element.26.powers, f32[240,128]{1,0:T(8,128)S(1)} %get-tuple-element.39.first, f32[240,128]{1,0:T(8,128)S(1)} %collective-permute-done.5.second), custom_call_target="tpu_custom_call" | custom-call | tf_op jit(solution)/shard_map/pallas_call | solution.py:657
  32.8 2.5 %collective-permute-done.8 = f32[200,128]{1,0:T(8,128)S(1)} collective-permute-done((f32[200,128]{1,0:T(8,128)S(1)}, f32[200,128]{1,0:T(8,128)S(1)}, u32[]{:S(2)}, u32[]{:S(2)}) %collective-permute-start.8) | collective-permute-done | bytes 102432 | tf_op jit(solution)/shard_map/ppermute | solution.py:536
  35.3 1.8 %collective-permute-start.10 = (f32[384,128]{1,0:T(8,128)S(1)}, f32[384,128]{1,0:T(8,128)S(1)}, u32[]{:S(2)}, u32[]{:S(2)}) collective-permute-start(f32[384,128]{1,0:T(8,128)S(1)} %shard_map.90), channel_id=1, source_target_pairs={{0,4},{4,0},{8,12},{12,8},{16,20},{20,16},{24,28},{28,24},{1,5},{5... | collective-permute-start | bytes 589832 | tf_op jit(solution)/shard_map/ppermute | solution.py:521
  37.2 2.6 %collective-permute-start.9 = (f32[200,128]{1,0:T(8,128)S(1)}, f32[200,128]{1,0:T(8,128)S(1)}, u32[]{:S(2)}, u32[]{:S(2)}) collective-permute-start(f32[200,128]{1,0:T(8,128)S(1)} %fusion.1), channel_id=1, source_target_pairs={{0,16},{1,3},{2,18},{3,1},{4,20},{5,7},{6,22},{7,5},{8,24},{9,11},... | collective-permute-start | bytes 307208 | tf_op jit(solution)/shard_map/ppermute | solution.py:536
  39.8 3.0 %collective-permute-done.9 = f32[200,128]{1,0:T(8,128)S(1)} collective-permute-done((f32[200,128]{1,0:T(8,128)S(1)}, f32[200,128]{1,0:T(8,128)S(1)}, u32[]{:S(2)}, u32[]{:S(2)}) %collective-permute-start.9) | collective-permute-done | bytes 102432 | tf_op jit(solution)/shard_map/ppermute | solution.py:536
  42.8 1.9 %collective-permute-start.12 = (f32[200,128]{1,0:T(8,128)S(1)}, f32[200,128]{1,0:T(8,128)S(1)}, u32[]{:S(2)}, u32[]{:S(2)}) collective-permute-start(f32[200,128]{1,0:T(8,128)S(1)} %add.47), channel_id=1, source_target_pairs={{0,8},{1,5},{2,10},{3,7},{4,12},{5,1},{6,14},{7,3},{8,0},{9,13},{1... | collective-permute-start | bytes 307208 | tf_op jit(solution)/shard_map/ppermute | solution.py:536
  44.7 0.2 collective-permute-start.11
  44.9 2.6 %collective-permute-done.12 = f32[200,128]{1,0:T(8,128)S(1)} collective-permute-done((f32[200,128]{1,0:T(8,128)S(1)}, f32[200,128]{1,0:T(8,128)S(1)}, u32[]{:S(2)}, u32[]{:S(2)}) %collective-permute-start.12) | collective-permute-done | bytes 102432 | tf_op jit(solution)/shard_map/ppermute | solution.py:536
  47.5 3.6 %collective-permute-start.15 = (f32[128,128]{1,0:T(8,128)S(1)}, f32[128,128]{1,0:T(8,128)S(1)}, u32[]{:S(2)}, u32[]{:S(2)}) collective-permute-start(f32[128,128]{1,0:T(8,128)S(1)} %get-tuple-element.37), channel_id=1, source_target_pairs={{0,6},{1,25},{2,4},{3,27},{4,2},{5,29},{6,0},{7,31},{8,14},{9,17},... | collective-permute-start | bytes 196616 | tf_op jit(solution)/shard_map/ppermute | solution.py:536
  51.1 0.6 %collective-permute-start.13 = (f32[128,128]{1,0:T(8,128)S(1)}, f32[128,128]{1,0:T(8,128)S(1)}, u32[]{:S(2)}, u32[]{:S(2)}) collective-permute-start(f32[128,128]{1,0:T(8,128)S(1)} %get-tuple-element.37), channel_id=1, source_target_pairs={{0,2},{1,17},{2,0},{3,19},{4,6},{5,21},{6,4},{7,23},{8,10},{9,25},... | collective-permute-start | bytes 196616 | tf_op jit(solution)/shard_map/ppermute | solution.py:536
  51.7 1.6 %shard_map.91 = f32[2,256,256]{2,1,0:T(8,128)} custom-call(s32[4]{0:T(128)S(1)} %pad_add_fusion.place, f32[2,256,256]{2,1,0:T(8,128)S(1)} %copy-done.1, f32[2,4,328,128]{3,2,1,0:T(8,128)S(1)} %get-tuple-element.27.work, f32[4,328,128]{2,1,0:T(8,128)S(1)} %get-tuple-element.26.powers, f32[240,128]{1,0:T(8,128)S(1)} %get-tuple-element.39.first, ...), custom_call_target="tpu_custom_call" | custom-call | tf_op jit(solution)/shard_map/pallas_call | solution.py:677
  53.4 2.0 %collective-permute-done.14 = f32[128,128]{1,0:T(8,128)S(1)} collective-permute-done((f32[128,128]{1,0:T(8,128)S(1)}, f32[128,128]{1,0:T(8,128)S(1)}, u32[]{:S(2)}, u32[]{:S(2)}) %collective-permute-start.14) | collective-permute-done | bytes 65568 | tf_op jit(solution)/shard_map/ppermute | solution.py:536
  55.5 1.5 %collective-permute-done.16 = f32[512,128]{1,0:T(8,128)S(1)} collective-permute-done((f32[512,128]{1,0:T(8,128)S(1)}, f32[512,128]{1,0:T(8,128)S(1)}, u32[]{:S(2)}, u32[]{:S(2)}) %collective-permute-start.16) | collective-permute-done | bytes 262176 | tf_op jit(solution)/shard_map/ppermute | solution.py:521
  57.0 1.7 %shard_map.92 = f32[2,256,256]{2,1,0:T(8,128)} custom-call(s32[4]{0:T(128)S(1)} %pad_add_fusion.place, f32[1024,128]{1,0:T(8,128)S(1)} %constant_dynamic-update-slice_fusion.stepped, f32[8,128]{1,0:T(8,128)S(1)} %slice.64.total), custom_call_target="tpu_custom_call" | custom-call | tf_op jit(solution)/shard_map/pallas_call | solution.py:685
  (45 shorter events, 0.6 us)
Async XLA Ops:
  1.5 8.3 %collective-permute-start.1 = (f32[2,32,256]{2,1,0:T(8,128)S(1)}, f32[2,32,256]{2,1,0:T(8,128)S(1)}, u32[]{:S(2)}, u32[]{:S(2)}) collective-permute-start(f32[2,32,256]{2,1,0:T(8,128)S(1)} %get-tuple-element.40), channel_id=1, source_target_pairs={{0,0},{4,8},{8,4},{12,16},{16,12},{20,24},{24,20},{28,28},{1,1},{5... | collective-permute-start | bytes 196616 | tf_op jit(solution)/shard_map/ppermute | solution.py:521
  2.2 8.0 %collective-permute-start = (f32[2,32,256]{2,1,0:T(8,128)S(1)}, f32[2,32,256]{2,1,0:T(8,128)S(1)}, u32[]{:S(2)}, u32[]{:S(2)}) collective-permute-start(f32[2,32,256]{2,1,0:T(8,128)S(1)} %get-tuple-element.41), channel_id=1, source_target_pairs={{0,4},{4,0},{8,12},{12,8},{16,20},{20,16},{24,28},{28,24},{1,5},{5... | collective-permute-start | bytes 196616 | tf_op jit(solution)/shard_map/ppermute | solution.py:521
  8.1 1.0 %copy-start = (f32[2,256,256]{2,1,0:T(8,128)S(1)}, f32[2,256,256]{2,1,0:T(8,128)}, u32[]{:S(2)}) copy-start(f32[2,256,256]{2,1,0:T(8,128)} %field.5) | copy-start | bytes 1572868
  10.9 1.5 %collective-permute-start.2 = (f32[4,80,128]{2,1,0:T(8,128)S(1)}, f32[4,80,128]{2,1,0:T(8,128)S(1)}, u32[]{:S(2)}, u32[]{:S(2)}) collective-permute-start(f32[4,80,128]{2,1,0:T(8,128)S(1)} %get-tuple-element.23), channel_id=1, source_target_pairs={{0,1},{1,0},{2,3},{3,2},{4,5},{5,4},{6,7},{7,6},{8,9},{9,8},{10,11... | collective-permute-start | bytes 491528 | tf_op jit(solution)/shard_map/ppermute | solution.py:521
  12.4 5.3 %collective-permute-start.3 = (f32[2,80,128]{2,1,0:T(8,128)S(1)}, f32[2,80,128]{2,1,0:T(8,128)S(1)}, u32[]{:S(2)}, u32[]{:S(2)}) collective-permute-start(f32[2,80,128]{2,1,0:T(8,128)S(1)} %slice.54), channel_id=1, source_target_pairs={{0,2},{1,0},{2,3},{3,1},{4,6},{5,4},{6,7},{7,5},{8,10},{9,8},{10,1... | collective-permute-start | bytes 245768 | tf_op jit(solution)/shard_map/ppermute | solution.py:528
  13.9 1.0 %copy-start.2 = (f32[2,256,256]{2,1,0:T(8,128)S(1)}, f32[2,256,256]{2,1,0:T(8,128)}, u32[]{:S(2)}) copy-start(f32[2,256,256]{2,1,0:T(8,128)} %probe.3) | copy-start | bytes 1572868
  14.9 1.2 %copy-start.6 = (f32[1,1,4,256,256]{4,3,2,1,0:T(8,128)S(1)}, f32[1,1,4,256,256]{4,3,2,1,0:T(8,128)}, u32[]{:S(2)}) copy-start(f32[1,1,4,256,256]{4,3,2,1,0:T(8,128)} %param.9) | copy-start | bytes 3145732
  16.1 1.6 %copy-start.1 = (f32[2,256,256]{2,1,0:T(8,128)S(1)}, f32[2,256,256]{2,1,0:T(8,128)}, u32[]{:S(2)}) copy-start(f32[2,256,256]{2,1,0:T(8,128)} %field.5) | copy-start | bytes 1572868
  16.1 1.6 %copy-start.3 = (bf16[2,2,256,256]{3,2,1,0:T(8,128)(2,1)S(1)}, bf16[2,2,256,256]{3,2,1,0:T(8,128)(2,1)}, u32[]{:S(2)}) copy-start(bf16[2,2,256,256]{3,2,1,0:T(8,128)(2,1)} %constant.31.clone.matrices) | copy-start | bytes 1572868
  16.1 1.6 %copy-start.4 = (f32[2,128,128]{2,1,0:T(8,128)S(1)}, f32[2,128,128]{2,1,0:T(8,128)}, u32[]{:S(2)}) copy-start(f32[2,128,128]{2,1,0:T(8,128)} %constant.32.clone.row_turn) | copy-start | bytes 393220
  16.1 1.6 %copy-start.5 = (f32[2,8,128]{2,1,0:T(8,128)S(1)}, f32[2,8,128]{2,1,0:T(8,128)}, u32[]{:S(2)}) copy-start(f32[2,8,128]{2,1,0:T(8,128)} %constant.33.clone.column_turn) | copy-start | bytes 24580
  24.5 2.1 %collective-permute-start.4 = (f32[1256,128]{1,0:T(8,128)S(1)}, f32[1256,128]{1,0:T(8,128)S(1)}, u32[]{:S(2)}, u32[]{:S(2)}) collective-permute-start(f32[1256,128]{1,0:T(8,128)S(1)} %get-tuple-element.28), channel_id=1, source_target_pairs={{0,1},{1,0},{2,3},{3,2},{4,5},{5,4},{6,7},{7,6},{8,9},{9,8},{10,11... | collective-permute-start | bytes 1929224 | tf_op jit(solution)/shard_map/ppermute | solution.py:521
  26.7 3.1 %collective-permute-start.5 = (f32[240,128]{1,0:T(8,128)S(1)}, f32[240,128]{1,0:T(8,128)S(1)}, u32[]{:S(2)}, u32[]{:S(2)}) collective-permute-start(f32[240,128]{1,0:T(8,128)S(1)} %get-tuple-element.38), channel_id=1, source_target_pairs={{0,2},{1,0},{2,3},{3,1},{4,6},{5,4},{6,7},{7,5},{8,10},{9,8},{10,1... | collective-permute-start | bytes 368648 | tf_op jit(solution)/shard_map/ppermute | solution.py:528
  27.4 5.4 %collective-permute-start.7 = (f32[200,128]{1,0:T(8,128)S(1)}, f32[200,128]{1,0:T(8,128)S(1)}, u32[]{:S(2)}, u32[]{:S(2)}) collective-permute-start(f32[200,128]{1,0:T(8,128)S(1)} %get-tuple-element.47), channel_id=1, source_target_pairs={{0,4},{1,9},{2,6},{3,11},{4,0},{5,13},{6,2},{7,15},{8,12},{9,1},{1... | collective-permute-start | bytes 307208 | tf_op jit(solution)/shard_map/ppermute | solution.py:536
  29.8 5.6 %collective-permute-start.8 = (f32[200,128]{1,0:T(8,128)S(1)}, f32[200,128]{1,0:T(8,128)S(1)}, u32[]{:S(2)}, u32[]{:S(2)}) collective-permute-start(f32[200,128]{1,0:T(8,128)S(1)} %concatenate.29), channel_id=1, source_target_pairs={{0,6},{1,25},{2,4},{3,27},{4,2},{5,29},{6,0},{7,31},{8,14},{9,17},... | collective-permute-start | bytes 307208 | tf_op jit(solution)/shard_map/ppermute | solution.py:536
  29.8 5.6 %collective-permute-start.6 = (f32[200,128]{1,0:T(8,128)S(1)}, f32[200,128]{1,0:T(8,128)S(1)}, u32[]{:S(2)}, u32[]{:S(2)}) collective-permute-start(f32[200,128]{1,0:T(8,128)S(1)} %get-tuple-element.31), channel_id=1, source_target_pairs={{0,2},{1,17},{2,0},{3,19},{4,6},{5,21},{6,4},{7,23},{8,10},{9,25},... | collective-permute-start | bytes 307208 | tf_op jit(solution)/shard_map/ppermute | solution.py:536
  35.3 7.4 %collective-permute-start.10 = (f32[384,128]{1,0:T(8,128)S(1)}, f32[384,128]{1,0:T(8,128)S(1)}, u32[]{:S(2)}, u32[]{:S(2)}) collective-permute-start(f32[384,128]{1,0:T(8,128)S(1)} %shard_map.90), channel_id=1, source_target_pairs={{0,4},{4,0},{8,12},{12,8},{16,20},{20,16},{24,28},{28,24},{1,5},{5... | collective-permute-start | bytes 589832 | tf_op jit(solution)/shard_map/ppermute | solution.py:521
  37.2 5.6 %collective-permute-start.9 = (f32[200,128]{1,0:T(8,128)S(1)}, f32[200,128]{1,0:T(8,128)S(1)}, u32[]{:S(2)}, u32[]{:S(2)}) collective-permute-start(f32[200,128]{1,0:T(8,128)S(1)} %fusion.1), channel_id=1, source_target_pairs={{0,16},{1,3},{2,18},{3,1},{4,20},{5,7},{6,22},{7,5},{8,24},{9,11},... | collective-permute-start | bytes 307208 | tf_op jit(solution)/shard_map/ppermute | solution.py:536
  42.8 4.7 %collective-permute-start.12 = (f32[200,128]{1,0:T(8,128)S(1)}, f32[200,128]{1,0:T(8,128)S(1)}, u32[]{:S(2)}, u32[]{:S(2)}) collective-permute-start(f32[200,128]{1,0:T(8,128)S(1)} %add.47), channel_id=1, source_target_pairs={{0,8},{1,5},{2,10},{3,7},{4,12},{5,1},{6,14},{7,3},{8,0},{9,13},{1... | collective-permute-start | bytes 307208 | tf_op jit(solution)/shard_map/ppermute | solution.py:536
  44.7 7.0 %collective-permute-start.11 = (f32[192,128]{1,0:T(8,128)S(1)}, f32[192,128]{1,0:T(8,128)S(1)}, u32[]{:S(2)}, u32[]{:S(2)}) collective-permute-start(f32[192,128]{1,0:T(8,128)S(1)} %get-tuple-element.45), channel_id=1, source_target_pairs={{0,8},{4,0},{8,16},{12,4},{16,24},{20,12},{24,28},{28,20},{1,9},{5... | collective-permute-start | bytes 294920 | tf_op jit(solution)/shard_map/ppermute | solution.py:528
  47.5 5.8 %collective-permute-start.15 = (f32[128,128]{1,0:T(8,128)S(1)}, f32[128,128]{1,0:T(8,128)S(1)}, u32[]{:S(2)}, u32[]{:S(2)}) collective-permute-start(f32[128,128]{1,0:T(8,128)S(1)} %get-tuple-element.37), channel_id=1, source_target_pairs={{0,6},{1,25},{2,4},{3,27},{4,2},{5,29},{6,0},{7,31},{8,14},{9,17},... | collective-permute-start | bytes 196616 | tf_op jit(solution)/shard_map/ppermute | solution.py:536
  51.1 4.3 %collective-permute-start.14 = (f32[128,128]{1,0:T(8,128)S(1)}, f32[128,128]{1,0:T(8,128)S(1)}, u32[]{:S(2)}, u32[]{:S(2)}) collective-permute-start(f32[128,128]{1,0:T(8,128)S(1)} %get-tuple-element.37), channel_id=1, source_target_pairs={{0,4},{1,9},{2,6},{3,11},{4,0},{5,13},{6,2},{7,15},{8,12},{9,1},{1... | collective-permute-start | bytes 196616 | tf_op jit(solution)/shard_map/ppermute | solution.py:536
  51.1 4.3 %collective-permute-start.13 = (f32[128,128]{1,0:T(8,128)S(1)}, f32[128,128]{1,0:T(8,128)S(1)}, u32[]{:S(2)}, u32[]{:S(2)}) collective-permute-start(f32[128,128]{1,0:T(8,128)S(1)} %get-tuple-element.37), channel_id=1, source_target_pairs={{0,2},{1,17},{2,0},{3,19},{4,6},{5,21},{6,4},{7,23},{8,10},{9,25},... | collective-permute-start | bytes 196616 | tf_op jit(solution)/shard_map/ppermute | solution.py:536
  55.4 1.6 %collective-permute-start.16 = (f32[512,128]{1,0:T(8,128)S(1)}, f32[512,128]{1,0:T(8,128)S(1)}, u32[]{:S(2)}, u32[]{:S(2)}) collective-permute-start(f32[512,128]{1,0:T(8,128)S(1)} %pad_maximum_fusion), channel_id=1, source_target_pairs={{0,1},{1,0},{2,3},{3,2},{4,5},{5,4},{6,7},{7,6},{8,9},{9,8},{10,11... | collective-permute-start | bytes 786440 | tf_op jit(solution)/shard_map/ppermute | solution.py:521
where the time goes:
time: 59.6 us; the launch traced here: 58.7 us
  starting transfers between devices  24.3 us (41%)
  waiting for transfers between devices  14.6 us (24%)
  Pallas kernels  13.6 us (23%)
  local copies, waits for them, and re-layouts  5.1 us (9%)
  between operations  0.88 us (1%)
    ppermute x8, starting transfers between devices, exchanged(): lax.ppermute(block, ('row', 'col'), [(i, i ^ masks[i % 2]) for i in range...  13.5 us
    ppermute x8, waiting for transfers between devices, exchanged(): lax.ppermute(block, ('row', 'col'), [(i, i ^ masks[i % 2]) for i in range...  10 us
    ppermute x6, starting transfers between devices, paired(): return lax.ppermute(block, axis, list(enumerate(target)))  8.49 us
    pallas_call x1, Pallas kernels, per_device(): call(functools.partial(frames_kernel, counts, blocks), (shape(2, side //...  6.78 us
    ppermute x6, waiting for transfers between devices, paired(): return lax.ppermute(block, axis, list(enumerate(target)))  4.56 us
    unnamed x17, local copies, waits for them, and re-layouts  3.34 us
    ppermute x3, starting transfers between devices, relayed(): return lax.ppermute(block, axis, list(target.items()))  2.33 us
    pallas_call x1, Pallas kernels, per_device(): call(functools.partial(probe_kernel, frame_count, blocks), shape(*probe.s...  1.67 us
  transfers between devices with their start and end apart: 17, of which 8 were waited for; matrix products, arithmetic and copies ran while one was open for 2% of the time, Pallas kernels for 8%

commit v1 on v0

--- a/solution.py
+++ b/solution.py
@@ -660,7 +660,6 @@
         scalars=1,
         operands=4,
     )(place, work, powers, first, second)
-    current, edges = lax.optimization_barrier((current, edges))
     edges = paired(edges, "row", 0)
     for step in range(halvings, len(orders[0])):
         if step == halvings + 1:

time: 59.6 us -> 58.7 us (0.985)
  waiting for transfers between devices: 14.6 us -> 12 us
  starting transfers between devices: 24.3 us -> 25.9 us
    ppermute x8, waiting for transfers between devices: 10 us -> 7.48 us  [exchanged(): lax.ppermute(block, ('row', 'col'), [(i, i ^ masks[i % 2]) for i in range...]
    ppermute x8, starting transfers between devices: 13.5 us -> 14.7 us  [exchanged(): lax.ppermute(block, ('row', 'col'), [(i, i ^ masks[i % 2]) for i in range...]
where the time goes in v1:
time: 58.7 us; the launch traced here: 57.8 us
  starting transfers between devices  25.9 us (44%)
  Pallas kernels  13.6 us (23%)
  waiting for transfers between devices  12 us (20%)
  local copies, waits for them, and re-layouts  5.1 us (9%)
  between operations  0.87 us (1%)
    ppermute x8, starting transfers between devices, exchanged(): lax.ppermute(block, ('row', 'col'), [(i, i ^ masks[i % 2]) for i in range...  14.7 us
    ppermute x6, starting transfers between devices, paired(): return lax.ppermute(block, axis, list(enumerate(target)))  9.06 us
    ppermute x8, waiting for transfers between devices, exchanged(): lax.ppermute(block, ('row', 'col'), [(i, i ^ masks[i % 2]) for i in range...  7.48 us
    pallas_call x1, Pallas kernels, per_device(): call(functools.partial(frames_kernel, counts, blocks), (shape(2, side //...  6.8 us
    ppermute x6, waiting for transfers between devices, paired(): return lax.ppermute(block, axis, list(enumerate(target)))  4.56 us
    unnamed x17, local copies, waits for them, and re-layouts  3.34 us
    ppermute x3, starting transfers between devices, relayed(): return lax.ppermute(block, axis, list(target.items()))  2.14 us
    pallas_call x1, Pallas kernels, per_device(): call(functools.partial(probe_kernel, frame_count, blocks), shape(*probe.s...  1.67 us
  transfers between devices with their start and end apart: 17, of which 8 were waited for; matrix products, arithmetic and copies ran while one was open for 2% of the time, Pallas kernels for 8%

profile of v1, /device:TPU:0, one launch (start us, length us, event | category | flops | bytes accessed | tf_op | source)
XLA Modules:
  0.0 57.8 jit_solution(520105294327568416)
XLA Ops:
  0.6 0.9 %constant_dynamic-slice_fusion = (f32[2,32,256]{2,1,0:T(8,128)S(1)}, f32[2,32,256]{2,1,0:T(8,128)S(1)}) fusion(f32[2,256,256]{2,1,0:T(8,128)} %field.5, s32[]{:T(128)S(6)} %select_n.16, s32[]{:T(128)S(6)} %select_n.15), kind=kLoop, calls=%fused_computation.14 | loop fusion | bytes 262152 | tf_op jit(solution)/shard_map/dynamic_slice | solution.py:581
  1.5 0.7 %collective-permute-start.1 = (f32[2,32,256]{2,1,0:T(8,128)S(1)}, f32[2,32,256]{2,1,0:T(8,128)S(1)}, u32[]{:S(2)}, u32[]{:S(2)}) collective-permute-start(f32[2,32,256]{2,1,0:T(8,128)S(1)} %get-tuple-element.36), channel_id=1, source_target_pairs={{0,0},{4,8},{8,4},{12,16},{16,12},{20,24},{24,20},{28,28},{1,1},{5... | collective-permute-start | bytes 196616 | tf_op jit(solution)/shard_map/ppermute | solution.py:521
  2.2 5.8 %collective-permute-start = (f32[2,32,256]{2,1,0:T(8,128)S(1)}, f32[2,32,256]{2,1,0:T(8,128)S(1)}, u32[]{:S(2)}, u32[]{:S(2)}) collective-permute-start(f32[2,32,256]{2,1,0:T(8,128)S(1)} %get-tuple-element.37), channel_id=1, source_target_pairs={{0,4},{4,0},{8,12},{12,8},{16,20},{20,16},{24,28},{28,24},{1,5},{5... | collective-permute-start | bytes 196616 | tf_op jit(solution)/shard_map/ppermute | solution.py:521
  8.1 1.0 %copy-done = f32[2,256,256]{2,1,0:T(8,128)S(1)} copy-done((f32[2,256,256]{2,1,0:T(8,128)S(1)}, f32[2,256,256]{2,1,0:T(8,128)}, u32[]{:S(2)}) %copy-start) | copy-done | bytes 524312
  9.1 0.7 %shard_map.86 = (f32[2,64,128]{2,1,0:T(8,128)S(1)}, f32[2,64,128]{2,1,0:T(8,128)S(1)}) custom-call(s32[4]{0:T(128)S(1)} %pad_add_fusion.place, f32[2,256,256]{2,1,0:T(8,128)S(1)} %copy-done), custom_call_target="tpu_custom_call" | custom-call | tf_op jit(solution)/shard_map/pallas_call | solution.py:584
  9.8 0.4 collective-permute-done.first
  10.2 0.6 %shard_map.87 = (f32[2,32,256]{2,1,0:T(8,128)S(1)}, f32[2,32,256]{2,1,0:T(8,128)S(1)}, f32[4,80,128]{2,1,0:T(8,128)S(1)}) custom-call(s32[4]{0:T(128)S(1)} %pad_add_fusion.place, f32[2,32,256]{2,1,0:T(8,128)S(1)} %collective-permute-done.first, f32[2,32,256]{2,1,0:T(8,128)S(1)} %collective-permute-done.1.second, ...), custom_call_target="tpu_custom_call" | custom-call | tf_op jit(solution)/shard_map/pallas_call | solution.py:587
  11.0 0.8 %copy.10.offsets = s32[4,2]{1,0:T(4,128)S(1)} copy(s32[4,2]{0,1:T(2,128)} %bitcast.7) | data formatting | bytes 64 | tf_op jit(solution)/shard_map/squeeze | solution.py:626
  11.7 0.6 %collective-permute-done.2.columns_first = f32[4,80,128]{2,1,0:T(8,128)S(1)} collective-permute-done((f32[4,80,128]{2,1,0:T(8,128)S(1)}, f32[4,80,128]{2,1,0:T(8,128)S(1)}, u32[]{:S(2)}, u32[]{:S(2)}) %collective-permute-start.2) | collective-permute-done | bytes 163872 | tf_op jit(solution)/shard_map/ppermute | solution.py:521
  12.4 1.5 %collective-permute-start.3 = (f32[2,80,128]{2,1,0:T(8,128)S(1)}, f32[2,80,128]{2,1,0:T(8,128)S(1)}, u32[]{:S(2)}, u32[]{:S(2)}) collective-permute-start(f32[2,80,128]{2,1,0:T(8,128)S(1)} %slice.54), channel_id=1, source_target_pairs={{0,2},{1,0},{2,3},{3,1},{4,6},{5,4},{6,7},{7,5},{8,10},{9,8},{10,1... | collective-permute-start | bytes 245768 | tf_op jit(solution)/shard_map/ppermute | solution.py:528
  13.9 1.0 %copy-done.2 = f32[2,256,256]{2,1,0:T(8,128)S(1)} copy-done((f32[2,256,256]{2,1,0:T(8,128)S(1)}, f32[2,256,256]{2,1,0:T(8,128)}, u32[]{:S(2)}) %copy-start.2) | copy-done | bytes 524312
  14.9 1.2 %copy-done.6 = f32[1,1,4,256,256]{4,3,2,1,0:T(8,128)S(1)} copy-done((f32[1,1,4,256,256]{4,3,2,1,0:T(8,128)S(1)}, f32[1,1,4,256,256]{4,3,2,1,0:T(8,128)}, u32[]{:S(2)}) %copy-start.6) | copy-done | bytes 1048600
  16.1 1.5 %shard_map.88 = (f32[4,512,128]{2,1,0:T(8,128)S(1)}, f32[8,128]{1,0:T(8,128)S(1)}, f32[4,328,128]{2,1,0:T(8,128)S(1)}) custom-call(s32[4,2]{1,0:T(4,128)S(1)} %copy.10.offsets, f32[4,256,256]{2,1,0:T(8,128)S(1)} %bitcast.6, f32[2,256,256]{2,1,0:T(8,128)S(1)} %copy-done.2), custom_call_target="tpu_custom_call" | custom-call | flops 1000000000 | bytes 2097152 | tf_op jit(solution)/shard_map/pallas_call | solution.py:596
  17.7 6.8 %shard_map.89 = (f32[2,4,328,128]{3,2,1,0:T(8,128)S(1)}, f32[776,128]{1,0:T(8,128)S(1)}, f32[1256,128]{1,0:T(8,128)S(1)}) custom-call(s32[4]{0:T(128)S(1)} %pad_add_fusion.place, s32[4,2]{1,0:T(4,128)S(1)} %copy.10.offsets, f32[2,256,256]{2,1,0:T(8,128)S(1)} %copy-done.1, f32[2,32,256]{2,1,0:T(8,128)S(1)} %get-tuple-element.19.above, ...), custom_call_target="tpu_custom_call" | custom-call | tf_op jit(solution)/shard_map/pallas_call | solution.py:611
  24.6 2.1 %collective-permute-done.4 = f32[1256,128]{1,0:T(8,128)S(1)} collective-permute-done((f32[1256,128]{1,0:T(8,128)S(1)}, f32[1256,128]{1,0:T(8,128)S(1)}, u32[]{:S(2)}, u32[]{:S(2)}) %collective-permute-start.4) | collective-permute-done | bytes 643104 | tf_op jit(solution)/shard_map/ppermute | solution.py:521
  26.7 0.6 collective-permute-start.5
  27.4 2.4 %collective-permute-start.7 = (f32[200,128]{1,0:T(8,128)S(1)}, f32[200,128]{1,0:T(8,128)S(1)}, u32[]{:S(2)}, u32[]{:S(2)}) collective-permute-start(f32[200,128]{1,0:T(8,128)S(1)} %get-tuple-element.43), channel_id=1, source_target_pairs={{0,4},{1,9},{2,6},{3,11},{4,0},{5,13},{6,2},{7,15},{8,12},{9,1},{1... | collective-permute-start | bytes 307208 | tf_op jit(solution)/shard_map/ppermute | solution.py:536
  29.8 2.4 %collective-permute-start.6 = (f32[200,128]{1,0:T(8,128)S(1)}, f32[200,128]{1,0:T(8,128)S(1)}, u32[]{:S(2)}, u32[]{:S(2)}) collective-permute-start(f32[200,128]{1,0:T(8,128)S(1)} %get-tuple-element.29), channel_id=1, source_target_pairs={{0,2},{1,17},{2,0},{3,19},{4,6},{5,21},{6,4},{7,23},{8,10},{9,25},... | collective-permute-start | bytes 307208 | tf_op jit(solution)/shard_map/ppermute | solution.py:536
  32.1 0.6 %shard_map.90 = f32[384,128]{1,0:T(8,128)S(1)} custom-call(s32[4]{0:T(128)S(1)} %pad_add_fusion.place, f32[2,4,328,128]{3,2,1,0:T(8,128)S(1)} %get-tuple-element.25.work, f32[4,328,128]{2,1,0:T(8,128)S(1)} %get-tuple-element.24.powers, f32[240,128]{1,0:T(8,128)S(1)} %get-tuple-element.35.first, f32[240,128]{1,0:T(8,128)S(1)} %collective-permute-done.5.second), custom_call_target="tpu_custom_call" | custom-call | tf_op jit(solution)/shard_map/pallas_call | solution.py:657
  32.8 2.4 %collective-permute-start.10 = (f32[384,128]{1,0:T(8,128)S(1)}, f32[384,128]{1,0:T(8,128)S(1)}, u32[]{:S(2)}, u32[]{:S(2)}) collective-permute-start(f32[384,128]{1,0:T(8,128)S(1)} %shard_map.90), channel_id=1, source_target_pairs={{0,4},{4,0},{8,12},{12,8},{16,20},{20,16},{24,28},{28,24},{1,5},{5... | collective-permute-start | bytes 589832 | tf_op jit(solution)/shard_map/ppermute | solution.py:521
  35.2 0.2 collective-permute-done.8
  35.4 2.9 %collective-permute-start.9 = (f32[200,128]{1,0:T(8,128)S(1)}, f32[200,128]{1,0:T(8,128)S(1)}, u32[]{:S(2)}, u32[]{:S(2)}) collective-permute-start(f32[200,128]{1,0:T(8,128)S(1)} %fusion.1), channel_id=1, source_target_pairs={{0,16},{1,3},{2,18},{3,1},{4,20},{5,7},{6,22},{7,5},{8,24},{9,11},... | collective-permute-start | bytes 307208 | tf_op jit(solution)/shard_map/ppermute | solution.py:536
  38.3 2.7 %collective-permute-done.9 = f32[200,128]{1,0:T(8,128)S(1)} collective-permute-done((f32[200,128]{1,0:T(8,128)S(1)}, f32[200,128]{1,0:T(8,128)S(1)}, u32[]{:S(2)}, u32[]{:S(2)}) %collective-permute-start.9) | collective-permute-done | bytes 102432 | tf_op jit(solution)/shard_map/ppermute | solution.py:536
  41.0 2.1 %collective-permute-start.12 = (f32[200,128]{1,0:T(8,128)S(1)}, f32[200,128]{1,0:T(8,128)S(1)}, u32[]{:S(2)}, u32[]{:S(2)}) collective-permute-start(f32[200,128]{1,0:T(8,128)S(1)} %add.47), channel_id=1, source_target_pairs={{0,8},{1,5},{2,10},{3,7},{4,12},{5,1},{6,14},{7,3},{8,0},{9,13},{1... | collective-permute-start | bytes 307208 | tf_op jit(solution)/shard_map/ppermute | solution.py:536
  43.1 0.1 collective-permute-start.11
  43.2 2.6 %collective-permute-done.12 = f32[200,128]{1,0:T(8,128)S(1)} collective-permute-done((f32[200,128]{1,0:T(8,128)S(1)}, f32[200,128]{1,0:T(8,128)S(1)}, u32[]{:S(2)}, u32[]{:S(2)}) %collective-permute-start.12) | collective-permute-done | bytes 102432 | tf_op jit(solution)/shard_map/ppermute | solution.py:536
  45.8 4.4 %collective-permute-start.15 = (f32[128,128]{1,0:T(8,128)S(1)}, f32[128,128]{1,0:T(8,128)S(1)}, u32[]{:S(2)}, u32[]{:S(2)}) collective-permute-start(f32[128,128]{1,0:T(8,128)S(1)} %get-tuple-element.33), channel_id=1, source_target_pairs={{0,6},{1,25},{2,4},{3,27},{4,2},{5,29},{6,0},{7,31},{8,14},{9,17},... | collective-permute-start | bytes 196616 | tf_op jit(solution)/shard_map/ppermute | solution.py:536
  50.2 0.6 %collective-permute-start.13 = (f32[128,128]{1,0:T(8,128)S(1)}, f32[128,128]{1,0:T(8,128)S(1)}, u32[]{:S(2)}, u32[]{:S(2)}) collective-permute-start(f32[128,128]{1,0:T(8,128)S(1)} %get-tuple-element.33), channel_id=1, source_target_pairs={{0,2},{1,17},{2,0},{3,19},{4,6},{5,21},{6,4},{7,23},{8,10},{9,25},... | collective-permute-start | bytes 196616 | tf_op jit(solution)/shard_map/ppermute | solution.py:536
  50.8 1.6 %shard_map.91 = f32[2,256,256]{2,1,0:T(8,128)} custom-call(s32[4]{0:T(128)S(1)} %pad_add_fusion.place, f32[2,256,256]{2,1,0:T(8,128)S(1)} %copy-done.1, f32[2,4,328,128]{3,2,1,0:T(8,128)S(1)} %get-tuple-element.25.work, f32[4,328,128]{2,1,0:T(8,128)S(1)} %get-tuple-element.24.powers, f32[240,128]{1,0:T(8,128)S(1)} %get-tuple-element.35.first, ...), custom_call_target="tpu_custom_call" | custom-call | tf_op jit(solution)/shard_map/pallas_call | solution.py:676
  52.5 2.0 %collective-permute-done.14 = f32[128,128]{1,0:T(8,128)S(1)} collective-permute-done((f32[128,128]{1,0:T(8,128)S(1)}, f32[128,128]{1,0:T(8,128)S(1)}, u32[]{:S(2)}, u32[]{:S(2)}) %collective-permute-start.14) | collective-permute-done | bytes 65568 | tf_op jit(solution)/shard_map/ppermute | solution.py:536
  54.6 1.5 %collective-permute-done.16 = f32[512,128]{1,0:T(8,128)S(1)} collective-permute-done((f32[512,128]{1,0:T(8,128)S(1)}, f32[512,128]{1,0:T(8,128)S(1)}, u32[]{:S(2)}, u32[]{:S(2)}) %collective-permute-start.16) | collective-permute-done | bytes 262176 | tf_op jit(solution)/shard_map/ppermute | solution.py:521
  56.1 1.7 %shard_map.92 = f32[2,256,256]{2,1,0:T(8,128)} custom-call(s32[4]{0:T(128)S(1)} %pad_add_fusion.place, f32[1024,128]{1,0:T(8,128)S(1)} %constant_dynamic-update-slice_fusion.stepped, f32[8,128]{1,0:T(8,128)S(1)} %slice.64.total), custom_call_target="tpu_custom_call" | custom-call | tf_op jit(solution)/shard_map/pallas_call | solution.py:684
  (45 shorter events, 0.6 us)
Async XLA Ops:
  1.5 8.3 %collective-permute-start.1 = (f32[2,32,256]{2,1,0:T(8,128)S(1)}, f32[2,32,256]{2,1,0:T(8,128)S(1)}, u32[]{:S(2)}, u32[]{:S(2)}) collective-permute-start(f32[2,32,256]{2,1,0:T(8,128)S(1)} %get-tuple-element.36), channel_id=1, source_target_pairs={{0,0},{4,8},{8,4},{12,16},{16,12},{20,24},{24,20},{28,28},{1,1},{5... | collective-permute-start | bytes 196616 | tf_op jit(solution)/shard_map/ppermute | solution.py:521
  2.2 8.0 %collective-permute-start = (f32[2,32,256]{2,1,0:T(8,128)S(1)}, f32[2,32,256]{2,1,0:T(8,128)S(1)}, u32[]{:S(2)}, u32[]{:S(2)}) collective-permute-start(f32[2,32,256]{2,1,0:T(8,128)S(1)} %get-tuple-element.37), channel_id=1, source_target_pairs={{0,4},{4,0},{8,12},{12,8},{16,20},{20,16},{24,28},{28,24},{1,5},{5... | collective-permute-start | bytes 196616 | tf_op jit(solution)/shard_map/ppermute | solution.py:521
  8.1 1.0 %copy-start = (f32[2,256,256]{2,1,0:T(8,128)S(1)}, f32[2,256,256]{2,1,0:T(8,128)}, u32[]{:S(2)}) copy-start(f32[2,256,256]{2,1,0:T(8,128)} %field.5) | copy-start | bytes 1572868
  10.9 1.5 %collective-permute-start.2 = (f32[4,80,128]{2,1,0:T(8,128)S(1)}, f32[4,80,128]{2,1,0:T(8,128)S(1)}, u32[]{:S(2)}, u32[]{:S(2)}) collective-permute-start(f32[4,80,128]{2,1,0:T(8,128)S(1)} %get-tuple-element.21), channel_id=1, source_target_pairs={{0,1},{1,0},{2,3},{3,2},{4,5},{5,4},{6,7},{7,6},{8,9},{9,8},{10,11... | collective-permute-start | bytes 491528 | tf_op jit(solution)/shard_map/ppermute | solution.py:521
  12.4 5.3 %collective-permute-start.3 = (f32[2,80,128]{2,1,0:T(8,128)S(1)}, f32[2,80,128]{2,1,0:T(8,128)S(1)}, u32[]{:S(2)}, u32[]{:S(2)}) collective-permute-start(f32[2,80,128]{2,1,0:T(8,128)S(1)} %slice.54), channel_id=1, source_target_pairs={{0,2},{1,0},{2,3},{3,1},{4,6},{5,4},{6,7},{7,5},{8,10},{9,8},{10,1... | collective-permute-start | bytes 245768 | tf_op jit(solution)/shard_map/ppermute | solution.py:528
  13.9 1.0 %copy-start.2 = (f32[2,256,256]{2,1,0:T(8,128)S(1)}, f32[2,256,256]{2,1,0:T(8,128)}, u32[]{:S(2)}) copy-start(f32[2,256,256]{2,1,0:T(8,128)} %probe.3) | copy-start | bytes 1572868
  14.9 1.2 %copy-start.6 = (f32[1,1,4,256,256]{4,3,2,1,0:T(8,128)S(1)}, f32[1,1,4,256,256]{4,3,2,1,0:T(8,128)}, u32[]{:S(2)}) copy-start(f32[1,1,4,256,256]{4,3,2,1,0:T(8,128)} %param.9) | copy-start | bytes 3145732
  16.1 1.6 %copy-start.1 = (f32[2,256,256]{2,1,0:T(8,128)S(1)}, f32[2,256,256]{2,1,0:T(8,128)}, u32[]{:S(2)}) copy-start(f32[2,256,256]{2,1,0:T(8,128)} %field.5) | copy-start | bytes 1572868
  16.1 1.6 %copy-start.3 = (bf16[2,2,256,256]{3,2,1,0:T(8,128)(2,1)S(1)}, bf16[2,2,256,256]{3,2,1,0:T(8,128)(2,1)}, u32[]{:S(2)}) copy-start(bf16[2,2,256,256]{3,2,1,0:T(8,128)(2,1)} %constant.31.clone.matrices) | copy-start | bytes 1572868
  16.1 1.6 %copy-start.4 = (f32[2,128,128]{2,1,0:T(8,128)S(1)}, f32[2,128,128]{2,1,0:T(8,128)}, u32[]{:S(2)}) copy-start(f32[2,128,128]{2,1,0:T(8,128)} %constant.32.clone.row_turn) | copy-start | bytes 393220
  16.1 1.6 %copy-start.5 = (f32[2,8,128]{2,1,0:T(8,128)S(1)}, f32[2,8,128]{2,1,0:T(8,128)}, u32[]{:S(2)}) copy-start(f32[2,8,128]{2,1,0:T(8,128)} %constant.33.clone.column_turn) | copy-start | bytes 24580
  24.5 2.1 %collective-permute-start.4 = (f32[1256,128]{1,0:T(8,128)S(1)}, f32[1256,128]{1,0:T(8,128)S(1)}, u32[]{:S(2)}, u32[]{:S(2)}) collective-permute-start(f32[1256,128]{1,0:T(8,128)S(1)} %get-tuple-element.26), channel_id=1, source_target_pairs={{0,1},{1,0},{2,3},{3,2},{4,5},{5,4},{6,7},{7,6},{8,9},{9,8},{10,11... | collective-permute-start | bytes 1929224 | tf_op jit(solution)/shard_map/ppermute | solution.py:521
  26.7 3.1 %collective-permute-start.5 = (f32[240,128]{1,0:T(8,128)S(1)}, f32[240,128]{1,0:T(8,128)S(1)}, u32[]{:S(2)}, u32[]{:S(2)}) collective-permute-start(f32[240,128]{1,0:T(8,128)S(1)} %get-tuple-element.34), channel_id=1, source_target_pairs={{0,2},{1,0},{2,3},{3,1},{4,6},{5,4},{6,7},{7,5},{8,10},{9,8},{10,1... | collective-permute-start | bytes 368648 | tf_op jit(solution)/shard_map/ppermute | solution.py:528
  27.4 7.8 %collective-permute-start.7 = (f32[200,128]{1,0:T(8,128)S(1)}, f32[200,128]{1,0:T(8,128)S(1)}, u32[]{:S(2)}, u32[]{:S(2)}) collective-permute-start(f32[200,128]{1,0:T(8,128)S(1)} %get-tuple-element.43), channel_id=1, source_target_pairs={{0,4},{1,9},{2,6},{3,11},{4,0},{5,13},{6,2},{7,15},{8,12},{9,1},{1... | collective-permute-start | bytes 307208 | tf_op jit(solution)/shard_map/ppermute | solution.py:536
  29.8 5.6 %collective-permute-start.8 = (f32[200,128]{1,0:T(8,128)S(1)}, f32[200,128]{1,0:T(8,128)S(1)}, u32[]{:S(2)}, u32[]{:S(2)}) collective-permute-start(f32[200,128]{1,0:T(8,128)S(1)} %concatenate.29), channel_id=1, source_target_pairs={{0,6},{1,25},{2,4},{3,27},{4,2},{5,29},{6,0},{7,31},{8,14},{9,17},... | collective-permute-start | bytes 307208 | tf_op jit(solution)/shard_map/ppermute | solution.py:536
  29.8 5.6 %collective-permute-start.6 = (f32[200,128]{1,0:T(8,128)S(1)}, f32[200,128]{1,0:T(8,128)S(1)}, u32[]{:S(2)}, u32[]{:S(2)}) collective-permute-start(f32[200,128]{1,0:T(8,128)S(1)} %get-tuple-element.29), channel_id=1, source_target_pairs={{0,2},{1,17},{2,0},{3,19},{4,6},{5,21},{6,4},{7,23},{8,10},{9,25},... | collective-permute-start | bytes 307208 | tf_op jit(solution)/shard_map/ppermute | solution.py:536
  32.8 8.2 %collective-permute-start.10 = (f32[384,128]{1,0:T(8,128)S(1)}, f32[384,128]{1,0:T(8,128)S(1)}, u32[]{:S(2)}, u32[]{:S(2)}) collective-permute-start(f32[384,128]{1,0:T(8,128)S(1)} %shard_map.90), channel_id=1, source_target_pairs={{0,4},{4,0},{8,12},{12,8},{16,20},{20,16},{24,28},{28,24},{1,5},{5... | collective-permute-start | bytes 589832 | tf_op jit(solution)/shard_map/ppermute | solution.py:521
  35.4 5.6 %collective-permute-start.9 = (f32[200,128]{1,0:T(8,128)S(1)}, f32[200,128]{1,0:T(8,128)S(1)}, u32[]{:S(2)}, u32[]{:S(2)}) collective-permute-start(f32[200,128]{1,0:T(8,128)S(1)} %fusion.1), channel_id=1, source_target_pairs={{0,16},{1,3},{2,18},{3,1},{4,20},{5,7},{6,22},{7,5},{8,24},{9,11},... | collective-permute-start | bytes 307208 | tf_op jit(solution)/shard_map/ppermute | solution.py:536
  41.0 4.7 %collective-permute-start.12 = (f32[200,128]{1,0:T(8,128)S(1)}, f32[200,128]{1,0:T(8,128)S(1)}, u32[]{:S(2)}, u32[]{:S(2)}) collective-permute-start(f32[200,128]{1,0:T(8,128)S(1)} %add.47), channel_id=1, source_target_pairs={{0,8},{1,5},{2,10},{3,7},{4,12},{5,1},{6,14},{7,3},{8,0},{9,13},{1... | collective-permute-start | bytes 307208 | tf_op jit(solution)/shard_map/ppermute | solution.py:536
  43.1 7.7 %collective-permute-start.11 = (f32[192,128]{1,0:T(8,128)S(1)}, f32[192,128]{1,0:T(8,128)S(1)}, u32[]{:S(2)}, u32[]{:S(2)}) collective-permute-start(f32[192,128]{1,0:T(8,128)S(1)} %get-tuple-element.41), channel_id=1, source_target_pairs={{0,8},{4,0},{8,16},{12,4},{16,24},{20,12},{24,28},{28,20},{1,9},{5... | collective-permute-start | bytes 294920 | tf_op jit(solution)/shard_map/ppermute | solution.py:528
  45.8 6.6 %collective-permute-start.15 = (f32[128,128]{1,0:T(8,128)S(1)}, f32[128,128]{1,0:T(8,128)S(1)}, u32[]{:S(2)}, u32[]{:S(2)}) collective-permute-start(f32[128,128]{1,0:T(8,128)S(1)} %get-tuple-element.33), channel_id=1, source_target_pairs={{0,6},{1,25},{2,4},{3,27},{4,2},{5,29},{6,0},{7,31},{8,14},{9,17},... | collective-permute-start | bytes 196616 | tf_op jit(solution)/shard_map/ppermute | solution.py:536
  50.2 4.3 %collective-permute-start.14 = (f32[128,128]{1,0:T(8,128)S(1)}, f32[128,128]{1,0:T(8,128)S(1)}, u32[]{:S(2)}, u32[]{:S(2)}) collective-permute-start(f32[128,128]{1,0:T(8,128)S(1)} %get-tuple-element.33), channel_id=1, source_target_pairs={{0,4},{1,9},{2,6},{3,11},{4,0},{5,13},{6,2},{7,15},{8,12},{9,1},{1... | collective-permute-start | bytes 196616 | tf_op jit(solution)/shard_map/ppermute | solution.py:536
  50.2 4.3 %collective-permute-start.13 = (f32[128,128]{1,0:T(8,128)S(1)}, f32[128,128]{1,0:T(8,128)S(1)}, u32[]{:S(2)}, u32[]{:S(2)}) collective-permute-start(f32[128,128]{1,0:T(8,128)S(1)} %get-tuple-element.33), channel_id=1, source_target_pairs={{0,2},{1,17},{2,0},{3,19},{4,6},{5,21},{6,4},{7,23},{8,10},{9,25},... | collective-permute-start | bytes 196616 | tf_op jit(solution)/shard_map/ppermute | solution.py:536
  54.5 1.6 %collective-permute-start.16 = (f32[512,128]{1,0:T(8,128)S(1)}, f32[512,128]{1,0:T(8,128)S(1)}, u32[]{:S(2)}, u32[]{:S(2)}) collective-permute-start(f32[512,128]{1,0:T(8,128)S(1)} %pad_maximum_fusion), channel_id=1, source_target_pairs={{0,1},{1,0},{2,3},{3,2},{4,5},{5,4},{6,7},{7,6},{8,9},{9,8},{10,11... | collective-permute-start | bytes 786440 | tf_op jit(solution)/shard_map/ppermute | solution.py:521
